TPU v7x, 32 devices: a whole 2x2x4 slice. The times are simulated.
32 devices in a mesh: fsdp: 8 (over z, x), dp: 4 (over y, core).
Axes of the slice: x: 2, y: 2, z: 4, core: 2. Of those that a mesh axis runs over, the one named last changes fastest.
Arguments:
- hidden_in: bfloat16 [64, 512, 1088], P(('fsdp', 'dp')), may hold values from -6 to 6
- cotangent: bfloat16 [64, 512, 1088], P(('fsdp', 'dp')), may hold values from -6 to 6
- lengths: int32 [64], P(('fsdp', 'dp')), may hold values from 1 to 512, as said below
- qkv_weight: float32 [1088, 3264], P('fsdp'), may hold values from -0.1875 to 0.1875
- qkv_mean: float32 [1088, 3264], P('fsdp'), may hold values from -40 to 40
- qkv_square: float32 [1088, 3264], P('fsdp'), may hold values from 3.41325 to 13.653
- out_weight: float32 [1088, 1088], P('fsdp'), may hold values from -0.75 to 0.75
- out_mean: float32 [1088, 1088], P('fsdp'), may hold values from -12 to 12
- out_square: float32 [1088, 1088], P('fsdp'), may hold values from 0.314019 to 1.22877
- up_weight: float32 [1088, 4352], P(None, 'fsdp'), may hold values from -0.1875 to 0.1875
- up_mean: float32 [1088, 4352], P(None, 'fsdp'), may hold values from -24 to 24
- up_square: float32 [1088, 4352], P(None, 'fsdp'), may hold values from 1.22877 to 4.91508
- down_weight: float32 [4352, 1088], P('fsdp'), may hold values from -0.09375 to 0.09375
- down_mean: float32 [4352, 1088], P('fsdp'), may hold values from -48 to 48
- down_square: float32 [4352, 1088], P('fsdp'), may hold values from 5.73426 to 23.2101
- vectors: float32 [8, 1088], P(None, 'fsdp'), may hold values from -1.2 to 1.4, as said below
- vectors_mean: float32 [8, 1088], P(None, 'fsdp'), may hold values from -64 to 64
- vectors_square: float32 [8, 1088], P(None, 'fsdp'), may hold values from 8.73792 to 35.4978
- upbias: float32 [4352], P('fsdp'), may hold values from -1.25 to 1.25
- upbias_mean: float32 [4352], P('fsdp'), may hold values from -24 to 24
- upbias_square: float32 [4352], P('fsdp'), may hold values from 1.22877 to 4.91508
Outputs:
- output: bfloat16 [64, 512, 1088], P(('fsdp', 'dp'))
- input_grad: float32 [64, 512, 1088], P(('fsdp', 'dp'))
- qkv_next: float32 [1088, 3264], P('fsdp')
- qkvmean_next: float32 [1088, 3264], P('fsdp')
- qkvsquare_next: float32 [1088, 3264], P('fsdp')
- out_next: float32 [1088, 1088], P('fsdp')
- outmean_next: float32 [1088, 1088], P('fsdp')
- outsquare_next: float32 [1088, 1088], P('fsdp')
- up_next: float32 [1088, 4352], P(None, 'fsdp')
- upmean_next: float32 [1088, 4352], P(None, 'fsdp')
- upsquare_next: float32 [1088, 4352], P(None, 'fsdp')
- down_next: float32 [4352, 1088], P('fsdp')
- downmean_next: float32 [4352, 1088], P('fsdp')
- downsquare_next: float32 [4352, 1088], P('fsdp')
- vectors_next: float32 [8, 1088], P(None, 'fsdp')
- vectorsmean_next: float32 [8, 1088], P(None, 'fsdp')
- vectorssquare_next: float32 [8, 1088], P(None, 'fsdp')
- upbias_next: float32 [4352], P('fsdp')
- upbiasmean_next: float32 [4352], P('fsdp')
- upbiassquare_next: float32 [4352], P('fsdp')
Inputs may be any that keep to these rules, and one draw needn't show every extreme that they name: `lengths`: every block holds one sequence of 1 to 512 tokens at its start; some block holds exactly 512. `vectors`: rows 0 and 5 are positive gains; the other rows are biases of both signs.
All inputs are finite; a program needn't handle non-finite values.
Results may differ from a plain program's by a relative error of at most 0.0095.
The roundings to bfloat16 on the way count: a program that leaves them out, or rounds other values in their place, can miss the bound.
Values may be sent and summed in bfloat16 or wider, within the bound.
No kernel may reach another device: no remote copies, remote signals or barrier semaphores. Data moves between devices by JAX's collectives and lax.ppermute only.
A program may use at most 320 MiB of HBM per device.

v0:
```python
import math

import jax
import jax.numpy as jnp
from jax import lax
from jax.sharding import PartitionSpec as P

D = 1088
HEADS = 17
HDIM = 64
BLOCK = 512
SLOTS = 2
STEP = 10


norm_eps = 1e-05
beta_first = 0.9
beta_second = 0.999
adam_floor = 1e-08
step_rates = (0.05, 0.2, 0.05, 0.03, 0.5, 0.3)
decay_rates = (0.1, 0.1, 0.1, 0.1, 0.0, 0.0)


def collect(shards):
    low_shards = tuple((member.astype(jnp.bfloat16) for member in shards))
    gathered = (
        lax.all_gather(low_shards[0], "fsdp", axis=0, tiled=True),
        lax.all_gather(low_shards[1], "fsdp", axis=0, tiled=True),
        lax.all_gather(low_shards[2], "fsdp", axis=1, tiled=True),
        lax.all_gather(low_shards[3], "fsdp", axis=0, tiled=True),
        lax.all_gather(low_shards[4], "fsdp", axis=1, tiled=True),
        lax.all_gather(low_shards[5], "fsdp", axis=0, tiled=True),
    )
    return (gathered[0], gathered[1], gathered[2], gathered[3], gathered[4], gathered[5])


def norm_forward(values, scales, offset):
    center = values - jnp.mean(values, axis=-1, keepdims=True)
    inverse = lax.rsqrt(jnp.mean(center * center, axis=-1, keepdims=True) + norm_eps)
    norm_hat = center * inverse
    return (norm_hat * scales + offset, norm_hat, inverse)


def norm_backward(gradient, norm_hat, inverse, scales):
    hat_grad = gradient * scales
    value_grad = inverse * (
        hat_grad
        - jnp.mean(hat_grad, axis=-1, keepdims=True)
        - norm_hat * jnp.mean(hat_grad * norm_hat, axis=-1, keepdims=True)
    )
    return (value_grad, jnp.sum(gradient * norm_hat, axis=0), jnp.sum(gradient, axis=0))


def causal_scores(queries, key_rows):
    scores = jnp.einsum("qhd,khd->hqk", queries, key_rows, preferred_element_type=jnp.float32) * (
        1.0 / math.sqrt(HDIM)
    )
    rows_at = lax.broadcasted_iota(jnp.int32, scores.shape, 1)
    cols_at = lax.broadcasted_iota(jnp.int32, scores.shape, 2)
    return jnp.where(rows_at >= cols_at, scores, -1e30)


def attend_forward(triple):
    queries, key_rows, values_in = triple
    scores = causal_scores(queries, key_rows)
    row_top = jnp.max(scores, axis=-1, keepdims=True)
    powers = jnp.exp(scores - row_top)
    row_total = jnp.sum(powers, axis=-1, keepdims=True)
    attn_probs = (powers / row_total).astype(jnp.bfloat16)
    context = jnp.einsum("hqk,khd->qhd", attn_probs, values_in, preferred_element_type=jnp.float32)
    return (context.astype(jnp.bfloat16), (row_top + jnp.log(row_total))[..., 0])


def attend_backward(pieces):
    queries, key_rows, values_in, logsum, context_grad = pieces
    scores = causal_scores(queries, key_rows)
    attn_probs = jnp.exp(scores - logsum[..., None])
    prob_grad = jnp.einsum(
        "qhd,khd->hqk", context_grad, values_in, preferred_element_type=jnp.float32
    )
    values_grad = jnp.einsum(
        "hqk,qhd->khd",
        attn_probs.astype(jnp.bfloat16),
        context_grad,
        preferred_element_type=jnp.float32,
    )
    inner_sum = jnp.sum(attn_probs * prob_grad, axis=-1, keepdims=True)
    score_grad = (attn_probs * (prob_grad - inner_sum)).astype(jnp.bfloat16)
    scale_factor = 1.0 / math.sqrt(HDIM)
    query_grad = (
        jnp.einsum("hqk,khd->qhd", score_grad, key_rows, preferred_element_type=jnp.float32)
        * scale_factor
    )
    keys_grad = (
        jnp.einsum("hqk,qhd->khd", score_grad, queries, preferred_element_type=jnp.float32)
        * scale_factor
    )
    return jnp.stack([query_grad, keys_grad, values_grad], axis=1).astype(jnp.bfloat16)


def adam_update(weight, mean_old, square_old, gradient, step_rate, decay_rate):
    mean_new = beta_first * mean_old + (1.0 - beta_first) * gradient
    square_new = beta_second * square_old + (1.0 - beta_second) * gradient * gradient
    mean_hat = mean_new / (1.0 - beta_first**STEP)
    square_hat = square_new / (1.0 - beta_second**STEP)
    weight_new = weight - step_rate * (
        mean_hat / (jnp.sqrt(square_hat) + adam_floor) + decay_rate * weight
    )
    return (weight_new, mean_new, square_new)


def per_device(
    hidden_in,
    cotangent,
    lengths,
    qkv_weight,
    qkv_mean,
    qkv_square,
    out_weight,
    out_mean,
    out_square,
    up_weight,
    up_mean,
    up_square,
    down_weight,
    down_mean,
    down_square,
    vectors,
    vectors_mean,
    vectors_square,
    upbias,
    upbias_mean,
    upbias_square,
):
    shards = (qkv_weight, out_weight, up_weight, down_weight, vectors, upbias)
    first_moments = (qkv_mean, out_mean, up_mean, down_mean, vectors_mean, upbias_mean)
    squares = (qkv_square, out_square, up_square, down_square, vectors_square, upbias_square)
    forward_params = collect(shards)
    qkv_full, out_full, up_full, down_full, vec_full, bias_full = forward_params
    vec_values = vec_full.astype(jnp.float32)
    row_count = SLOTS * BLOCK
    flat_in = hidden_in.reshape(row_count, D).astype(jnp.float32)
    positions = jnp.arange(BLOCK, dtype=jnp.int32)
    row_valid = (positions[None, :] < lengths[:, None]).astype(jnp.float32).reshape(row_count, 1)
    normed_one, hat_one, inv_one = norm_forward(flat_in, vec_values[0], vec_values[1])
    normed_low = normed_one.astype(jnp.bfloat16)
    bias_row = jnp.concatenate([vec_values[2], jnp.zeros((D,), jnp.float32), vec_values[3]])
    qkv_rows = (
        jnp.dot(normed_low, qkv_full, preferred_element_type=jnp.float32) + bias_row
    ).astype(jnp.bfloat16)
    qkv_split = qkv_rows.reshape(SLOTS, BLOCK, 3, HEADS, HDIM)
    queries = qkv_split[:, :, 0]
    key_rows = qkv_split[:, :, 1]
    values_in = qkv_split[:, :, 2]
    context, logsum = lax.map(attend_forward, (queries, key_rows, values_in))
    context_flat = context.reshape(row_count, D)
    residual = (
        flat_in
        + jnp.dot(context_flat, out_full, preferred_element_type=jnp.float32)
        + vec_values[4]
    )
    normed_two, hat_two, inv_two = norm_forward(residual, vec_values[5], vec_values[6])
    second_low = normed_two.astype(jnp.bfloat16)
    up_pre = jnp.dot(second_low, up_full, preferred_element_type=jnp.float32) + bias_full.astype(
        jnp.float32
    )
    active, gelu_back = jax.vjp(lambda pre_act: jax.nn.gelu(pre_act, approximate=True), up_pre)
    active_low = active.astype(jnp.bfloat16)
    down_out = jnp.dot(active_low, down_full, preferred_element_type=jnp.float32) + vec_values[7]
    output = ((residual + down_out) * row_valid).astype(jnp.bfloat16).reshape(SLOTS, BLOCK, D)
    backward_params = collect(shards)
    qkv_full, out_full, up_full, down_full, vec_full, bias_full = backward_params
    vec_values = vec_full.astype(jnp.float32)
    grad_out = cotangent.reshape(row_count, D).astype(jnp.float32) * row_valid
    grad_low = grad_out.astype(jnp.bfloat16)
    down_grad = jnp.einsum("nf,nd->fd", active_low, grad_low, preferred_element_type=jnp.float32)
    down_bias_grad = jnp.sum(grad_out, axis=0)
    active_grad = jnp.einsum("nd,fd->nf", grad_low, down_full, preferred_element_type=jnp.float32)
    up_low = gelu_back(active_grad)[0].astype(jnp.bfloat16)
    up_grad = jnp.einsum("nd,nf->df", second_low, up_low, preferred_element_type=jnp.float32)
    upbias_grad = jnp.sum(up_low.astype(jnp.float32), axis=0)
    second_grad = jnp.einsum("nf,df->nd", up_low, up_full, preferred_element_type=jnp.float32)
    resid_norm_grad, scale_two_grad, offset_two_grad = norm_backward(
        second_grad, hat_two, inv_two, vec_values[5]
    )
    resid_grad = grad_out + resid_norm_grad
    branch_low = resid_grad.astype(jnp.bfloat16)
    out_grad = jnp.einsum("nd,ne->de", context_flat, branch_low, preferred_element_type=jnp.float32)
    out_bias_grad = jnp.sum(branch_low.astype(jnp.float32), axis=0)
    context_grad = jnp.einsum(
        "ne,de->nd", branch_low, out_full, preferred_element_type=jnp.float32
    ).astype(jnp.bfloat16)
    context_grad = context_grad.reshape(SLOTS, BLOCK, HEADS, HDIM)
    qkv_rows_grad = lax.map(attend_backward, (queries, key_rows, values_in, logsum, context_grad))
    qkv_rows_grad = qkv_rows_grad.reshape(row_count, 3 * D)
    qkv_grad = jnp.einsum(
        "nd,ne->de", normed_low, qkv_rows_grad, preferred_element_type=jnp.float32
    )
    qkv_sums = jnp.sum(qkv_rows_grad.astype(jnp.float32), axis=0)
    normed_grad = jnp.einsum(
        "ne,de->nd", qkv_rows_grad, qkv_full, preferred_element_type=jnp.float32
    )
    input_norm_grad, scale_one_grad, offset_one_grad = norm_backward(
        normed_grad, hat_one, inv_one, vec_values[0]
    )
    input_grad = (resid_grad + input_norm_grad).reshape(SLOTS, BLOCK, D)
    vec_grad = jnp.stack(
        [
            scale_one_grad,
            offset_one_grad,
            qkv_sums[:D],
            qkv_sums[2 * D :],
            out_bias_grad,
            scale_two_grad,
            offset_two_grad,
            down_bias_grad,
        ]
    )
    shard_count = lax.axis_size("fsdp")
    bias_two = upbias_grad.reshape(shard_count, -1)
    split_part = (
        lax.psum_scatter(qkv_grad, "dp", scatter_dimension=1, tiled=True),
        lax.psum_scatter(out_grad, "dp", scatter_dimension=1, tiled=True),
        lax.psum_scatter(up_grad, "dp", scatter_dimension=0, tiled=True),
        lax.psum_scatter(down_grad, "dp", scatter_dimension=1, tiled=True),
        lax.psum_scatter(vec_grad, "dp", scatter_dimension=0, tiled=True),
        lax.psum_scatter(bias_two, "dp", scatter_dimension=1, tiled=True),
    )
    owner_part = (
        lax.psum_scatter(split_part[0], "fsdp", scatter_dimension=0, tiled=True),
        lax.psum_scatter(split_part[1], "fsdp", scatter_dimension=0, tiled=True),
        lax.psum_scatter(split_part[2], "fsdp", scatter_dimension=1, tiled=True),
        lax.psum_scatter(split_part[3], "fsdp", scatter_dimension=0, tiled=True),
        lax.psum_scatter(split_part[4], "fsdp", scatter_dimension=1, tiled=True),
        lax.psum_scatter(split_part[5], "fsdp", scatter_dimension=0, tiled=True),
    )
    joined = (
        lax.all_gather(owner_part[0], "dp", axis=1, tiled=True),
        lax.all_gather(owner_part[1], "dp", axis=1, tiled=True),
        lax.all_gather(owner_part[2], "dp", axis=0, tiled=True),
        lax.all_gather(owner_part[3], "dp", axis=1, tiled=True),
        lax.all_gather(owner_part[4], "dp", axis=0, tiled=True),
        lax.all_gather(owner_part[5], "dp", axis=1, tiled=True),
    )
    reduced = (joined[0], joined[1], joined[2], joined[3], joined[4], joined[5].reshape(-1))
    updates = []
    for group_index in range(6):
        updates.extend(
            adam_update(
                shards[group_index],
                first_moments[group_index],
                squares[group_index],
                reduced[group_index],
                step_rates[group_index],
                decay_rates[group_index],
            )
        )
    return (
        output,
        input_grad,
        updates[0],
        updates[1],
        updates[2],
        updates[3],
        updates[4],
        updates[5],
        updates[6],
        updates[7],
        updates[8],
        updates[9],
        updates[10],
        updates[11],
        updates[12],
        updates[13],
        updates[14],
        updates[15],
        updates[16],
        updates[17],
    )


def solution(mesh):
    placed = (
        P(("fsdp", "dp"), None, None),
        P(("fsdp", "dp"), None, None),
        P(("fsdp", "dp")),
        P("fsdp", None),
        P("fsdp", None),
        P("fsdp", None),
        P("fsdp", None),
        P("fsdp", None),
        P("fsdp", None),
        P(None, "fsdp"),
        P(None, "fsdp"),
        P(None, "fsdp"),
        P("fsdp", None),
        P("fsdp", None),
        P("fsdp", None),
        P(None, "fsdp"),
        P(None, "fsdp"),
        P(None, "fsdp"),
        P("fsdp"),
        P("fsdp"),
        P("fsdp"),
    )
    return jax.shard_map(
        per_device,
        mesh=mesh,
        in_specs=placed,
        out_specs=(
            P(("fsdp", "dp"), None, None),
            P(("fsdp", "dp"), None, None),
            P("fsdp", None),
            P("fsdp", None),
            P("fsdp", None),
            P("fsdp", None),
            P("fsdp", None),
            P("fsdp", None),
            P(None, "fsdp"),
            P(None, "fsdp"),
            P(None, "fsdp"),
            P("fsdp", None),
            P("fsdp", None),
            P("fsdp", None),
            P(None, "fsdp"),
            P(None, "fsdp"),
            P(None, "fsdp"),
            P("fsdp"),
            P("fsdp"),
            P("fsdp"),
        ),
        check_vma=False,
    )
```

profile of v0, /device:TPU:0, one launch (start us, length us, event | category | flops | bytes accessed | tf_op | source)
XLA Modules:
  0.0 1617.5 jit_solution(4393789467857137755)
XLA Ops:
  21.0 32.8 %all-gather = bf16[8,136,8]{1,2,0:T(8,128)(2,1)S(1)} all-gather(bf16[1,136,8]{1,2,0:T(8,128)(2,1)S(1)} %convert_bitcast_fusion.2), channel_id=1, replica_groups=mesh['fsdp'=8,'dp'=4] {'fsdp'}, dimensions={0}, use_global_device_ids=true | all-gather | bytes 19584 | tf_op jit(solution)/shard_map/all_gather | solution.py:31
  63.1 38.4 %all-reduce = bf16[4352]{0:T(1024)(128)(2,1)S(1)} all-reduce(bf16[4352]{0:T(1024)(128)(2,1)S(1)} %dynamic-update-slice), channel_id=1, replica_groups=mesh['fsdp'=8,'dp'=4] {'fsdp'}, use_global_device_ids=true, to_apply=%add | all-reduce | flops 4352 | bytes 17408
  113.6 12.2 all-gather.12.cloned.1.call-done
  125.8 15.4 add_convert_fusion
  141.2 15.9 reshape.256
  168.0 56.3 %while.22 = (s32[]{:T(128)}, bf16[2,512,17,64]{1,3,2,0:T(8,128)(2,1)}, f32[2,17,512]{2,1,0:T(8,128)S(1)}, bf16[2,512,17,64]{1,3,2,0:T(8,128)(2,1)}, bf16[2,512,1...) while((s32[]{:T(128)}, bf16[2,512,17,64]{1,3,2,0:T(8,128)(2,1)}, ...), condition=%wide.region_5.6_spmd, body=%wide.region_2.5_spmd.sunk | while | flops 1208245760 | bytes 58257496 | solution.py:155
  240.8 86.2 %all-gather.16.cloned.1.call-done = bf16[1088,4352]{0,1:T(8,128)(2,1)} async-done(((bf16[1088,544]{0,1:T(8,128)(2,1)}), bf16[1088,4352]{0,1:T(8,128)(2,1)}) %all-gather.16.cloned.1.call-update) | async-done | bytes 9469968 | tf_op jit(solution)/shard_map/all_gather | solution.py:29
  327.0 21.5 %fusion.86 = f32[1024,4352]{1,0:T(8,128)} fusion(bf16[1088,4352]{0,1:T(8,128)(2,1)} %all-gather.16.cloned.1.call-done, f32[1024,1088]{0,1:T(8,128)} %copy-done.7, f32[1088]{0:T(1024)S(1)} %copy-done.39, f32[1088]{0:T(1024)S(1)} %copy-done.17, f32[1024]{0:T(1024)S(1)} %add_rsqrt_fusion, f32[1024]{0:T(1024)S(1)} %broadcast_multiply_fusion.4), kind=kOutput, calls=%fused_computation.171 | convolution fusion | flops 9702801408 | bytes 31769088 | tf_op jit(solution)/shard_map/dot_general | solution.py:164
  348.4 124.6 %all-gather.18.cloned.1.call-done = bf16[4352,1088]{1,0:T(8,128)(2,1)} async-done(((bf16[544,1088]{1,0:T(8,128)(2,1)}), bf16[4352,1088]{1,0:T(8,128)(2,1)}) %all-gather.18.cloned.1.call-update) | async-done | bytes 9469968 | tf_op jit(solution)/shard_map/all_gather | solution.py:30
  473.0 29.2 %convert_reduce_fusion = (f32[4352]{0:T(1024)}, bf16[1024,4352]{1,0:T(8,128)(2,1)}) fusion(f32[1024,4352]{1,0:T(8,128)} %fusion.86, f32[4352]{0:T(1024)S(1)} %copy-done.23, bf16[4352,1088]{1,0:T(8,128)(2,1)} %all-gather.18.cloned.1.call-done, f32[1024,1088]{0,1:T(8,128)} %bitcast.217, f32[1024]{0:T(1024)S(1)} %bitcast.238), kind=kOutput, calls=%fused_computation.65 | convolution fusion | flops 9801953280 | bytes 40704000 | tf_op jit(solution)/shard_map/nd,fd->nf/dot_general | solution.py:178
  502.2 19.7 %multiply_reduce_fusion.1 = (f32[1088]{0:T(1024)}, f32[1024]{0:T(1024)S(1)}, f32[1024]{0:T(1024)S(1)}, f32[1088]{0:T(1024)}, f32[1024,1088]{0,1:T(8,128)}) fusion(f32[1024,1088]{0,1:T(8,128)} %copy-done.7, f32[1024]{0:T(1024)S(1)} %add_rsqrt_fusion, f32[1024]{0:T(1024)S(1)} %broadcast_multiply_fusion.4, f32[1088]{0:T(1024)S(1)} %copy-done.17, ...), kind=kOutput, calls=%fused_computation.87 | convolution fusion | flops 9707253760 | bytes 27325184 | tf_op jit(solution)/shard_map/nf,df->nd/dot_general | solution.py:182
  547.3 103.0 %while.23 = (s32[]{:T(128)}, bf16[2,512,3,17,64]{1,4,3,2,0:T(8,128)(2,1)}, bf16[2,512,17,64]{1,3,2,0:T(8,128)(2,1)}, bf16[2,512,17,64]{1,3,2,0:T(8,128)(2,1)}, f...) while((s32[]{:T(128)}, ...), condition=%wide.region_12.13_spmd, body=%wide.region_10.12_spmd.sunk | while | flops 2909494784 | bytes 187361488 | solution.py:194
  547.8 11.5 fusion.146
  559.3 12.7 multiply_reduce_fusion.9
  581.0 12.6 multiply_convert_fusion.12
  610.0 12.7 multiply_reduce_fusion.9
  631.5 12.4 multiply_convert_fusion.12
  650.4 12.8 copy.145
  668.1 11.4 fusion.100
  680.3 20.3 %fusion.85 = f32[1088,4352]{1,0:T(8,128)} fusion(bf16[1024,4352]{1,0:T(8,128)(2,1)} %get-tuple-element.293, f32[1024,1088]{0,1:T(8,128)} %copy-done.7, f32[1088]{0:T(1024)S(1)} %copy-done.40, f32[1088]{0:T(1024)S(1)} %copy-done.18, f32[1024]{0:T(1024)S(1)} %copy-done.33, f32[1024]{0:T(1024)S(1)} %copy-done.16), kind=kOutput, calls=%fused_computation.170 | convolution fusion | flops 9702801408 | bytes 32326144 | tf_op jit(solution)/shard_map/nd,nf->df/dot_general | solution.py:180
  701.3 20.1 %fusion.73 = f32[4352,1088]{0,1:T(8,128)} fusion(f32[1024,1088]{0,1:T(8,128)} %bitcast.219, f32[1024]{0:T(1024)S(1)} %bitcast.240, f32[1024,4352]{1,0:T(8,128)} %fusion.86, f32[4352]{0:T(1024)S(1)} %copy-done.24), kind=kOutput, calls=%fused_computation.126 | convolution fusion | flops 9744023552 | bytes 41243648 | tf_op jit(solution)/shard_map/nf,nd->fd/dot_general | solution.py:176
  721.5 72.6 %reduce-scatter.15.cloned.1.call-done = f32[1088,816]{0,1:T(8,128)} async-done(((f32[1088,3264]{0,1:T(8,128)}), f32[1088,816]{0,1:T(8,128)}) %reduce-scatter.15.cloned.1.call-update) | async-done | bytes 3551248 | tf_op jit(solution)/shard_map/reduce_scatter | solution.py:222
  794.1 142.6 %reduce-scatter.19.cloned.1.call-done = f32[272,4352]{1,0:T(8,128)} async-done(((f32[1088,4352]{1,0:T(8,128)}), f32[272,4352]{1,0:T(8,128)}) %reduce-scatter.19.cloned.1.call-update) | async-done | bytes 4734992 | tf_op jit(solution)/shard_map/reduce_scatter | solution.py:224
  943.2 136.1 %reduce-scatter.21.cloned.1.call-done = f32[4352,272]{0,1:T(8,128)} async-done(((f32[4352,1088]{0,1:T(8,128)}), f32[4352,272]{0,1:T(8,128)}) %reduce-scatter.21.cloned.1.call-update) | async-done | bytes 4734992 | tf_op jit(solution)/shard_map/reduce_scatter | solution.py:225
  1111.1 150.2 %all-reduce.13.cloned.1.call-done = (f32[1088,816]{0,1:T(8,128)}, f32[1088,272]{0,1:T(8,128)}) async-done(((f32[1088,816]{0,1:T(8,128)}, f32[1088,272]{0,1:T(8,128)}), (f32[1088,816]{0,1:T(8,128)}, f32[1088,272]{0,1:T(8,128)})) %all-reduce.13.cloned.1.call-update) | async-done | bytes 4734992
  1266.1 24.9 %fusion.64 = bf16[1024,1088]{0,1:T(8,128)(2,1)} fusion(f32[1024,1088]{0,1:T(8,128)} %copy-done.7, bf16[4352,1088]{1,0:T(8,128)(2,1)} %all-gather.18.cloned.1.call-done, f32[1024]{0:T(1024)S(1)} %bitcast.241, f32[1088]{0:T(1024)S(1)} %copy-done.38, f32[1024,4352]{1,0:T(8,128)} %fusion.86, f32[4352]{0:T(1024)S(1)} %copy-done.24), kind=kOutput, calls=%fused_computation.104 | convolution fusion | flops 9746251776 | bytes 34006272 | tf_op jit(solution)/shard_map/dot_general | solution.py:169
  1294.3 14.5 multiply_reduce_fusion.2
  1308.8 79.0 %reduce-scatter.23.cloned.1.call-done = f32[544,272]{1,0:T(8,128)} async-done(((f32[4352,272]{1,0:T(8,128)}), f32[544,272]{1,0:T(8,128)}) %reduce-scatter.23.cloned.1.call-update) | async-done | bytes 591888
  1400.5 11.5 all-reduce.10
  1412.2 38.7 %all-reduce.8 = (f32[2,1088]{1,0:T(2,128)S(1)}, f32[8,136]{1,0:T(8,128)S(1)}) all-reduce(f32[2,1088]{1,0:T(2,128)S(1)} %constant_dynamic-slice_fusion.2, f32[8,136]{1,0:T(8,128)S(1)} %constant_dynamic-slice_fusion.1), channel_id=11, replica_groups=mesh['fsdp'=8,'dp'=4] {'fsdp'}, use_global_device_ids=true, to_apply=%region_31.32.clone | all-reduce | flops 3264 | bytes 26112
  1466.0 49.2 %reduce-scatter.25.cloned.1.call-done = f32[544,272]{1,0:T(8,128)} async-done(((f32[4352,272]{1,0:T(8,128)}), f32[544,272]{1,0:T(8,128)}) %reduce-scatter.25.cloned.1.call-update) | async-done | bytes 591888
  1551.3 15.6 all-gather.20.cloned.1.call-done
  (274 shorter events, 341.1 us)
Async XLA Ops:
  7.2 118.6 %all-gather.12.cloned.1.call-start = ((), (), s32[]{:S(2)}) async-start(), calls=%async_computation.6 | async-start | bytes 8146944 | tf_op jit(solution)/shard_map/all_gather | solution.py:27
  9.8 221.2 %all-gather.14.cloned.1.call-start = ((), (), s32[]{:S(2)}) async-start(), calls=%async_computation.7 | async-start | bytes 2820096 | tf_op jit(solution)/shard_map/all_gather | solution.py:28
  11.7 315.3 %all-gather.16.cloned.1.call-start = ((), (), s32[]{:S(2)}) async-start(), calls=%async_computation.8 | async-start | bytes 11280384 | tf_op jit(solution)/shard_map/all_gather | solution.py:29
  14.8 458.2 %all-gather.18.cloned.1.call-start = ((), (), s32[]{:S(2)}) async-start(), calls=%async_computation.9 | async-start | bytes 11280384 | tf_op jit(solution)/shard_map/all_gather | solution.py:30
  17.7 703.8 %reduce-scatter.17.cloned.1.call-start = ((), (), s32[]{:S(2)}) async-start(), calls=%async_computation.11 | async-start | bytes 6266880 | tf_op jit(solution)/shard_map/reduce_scatter | solution.py:223
  54.5 71.3 %copy-start.13 = (f32[1088]{0:T(1024)}, f32[1088]{0:T(1024)S(1)}, u32[]{:S(2)}) copy-start(f32[1088]{0:T(1024)S(1)} %get-tuple-element.216) | copy-start | bytes 13060
  60.2 65.5 %copy-start.25 = (f32[1,4,2,128]{3,1,2,0:T(4,128)}, f32[1,4,2,128]{3,1,2,0:T(4,128)S(1)}, u32[]{:S(2)}) copy-start(f32[1,4,2,128]{3,1,2,0:T(4,128)S(1)} %copy.191) | copy-start | bytes 12292
  60.3 65.5 %copy-start.27 = (f32[1,4,2,128]{3,1,2,0:T(4,128)}, f32[1,4,2,128]{3,1,2,0:T(4,128)S(1)}, u32[]{:S(2)}) copy-start(f32[1,4,2,128]{3,1,2,0:T(4,128)S(1)} %copy.190) | copy-start | bytes 12292
  238.1 88.8 %copy-start.17 = (f32[1088]{0:T(1024)S(1)}, f32[1088]{0:T(1024)}, u32[]{:S(2)}) copy-start(f32[1088]{0:T(1024)} %get-tuple-element.209) | copy-start | bytes 13060
  238.1 88.8 %copy-start.39 = (f32[1088]{0:T(1024)S(1)}, f32[1088]{0:T(1024)}, u32[]{:S(2)}) copy-start(f32[1088]{0:T(1024)} %get-tuple-element.211) | copy-start | bytes 13060
  238.2 283.7 %copy-start.15 = (f32[1024]{0:T(1024)}, f32[1024]{0:T(1024)S(1)}, u32[]{:S(2)}) copy-start(f32[1024]{0:T(1024)S(1)} %broadcast_multiply_fusion.4) | copy-start | bytes 12292
  240.8 281.1 %copy-start.32 = (f32[1024]{0:T(1024)}, f32[1024]{0:T(1024)S(1)}, u32[]{:S(2)}) copy-start(f32[1024]{0:T(1024)S(1)} %add_rsqrt_fusion) | copy-start | bytes 12292
  326.9 146.1 %copy-start.23 = (f32[4352]{0:T(1024)S(1)}, f32[4352]{0:T(1024)}, u32[]{:S(2)}) copy-start(f32[4352]{0:T(1024)} %convert_element_type.140) | copy-start | bytes 52228
  326.9 146.1 %copy-start.29 = (f32[1,4,2,128]{3,1,2,0:T(4,128)S(1)}, f32[1,4,2,128]{3,1,2,0:T(4,128)}, u32[]{:S(2)}) copy-start(f32[1,4,2,128]{3,1,2,0:T(4,128)} %copy.193) | copy-start | bytes 12292
  547.3 246.8 %reduce-scatter.15.cloned.1.call-start = ((), (), s32[]{:S(2)}) async-start(), calls=%async_computation.10 | async-start | bytes 18800640 | tf_op jit(solution)/shard_map/reduce_scatter | solution.py:222
  679.6 257.2 %reduce-scatter.19.cloned.1.call-start = ((), (), s32[]{:S(2)}) async-start(), calls=%async_computation.12 | async-start | bytes 23674880 | tf_op jit(solution)/shard_map/reduce_scatter | solution.py:224
  700.6 378.7 %reduce-scatter.21.cloned.1.call-start = ((), (), s32[]{:S(2)}) async-start(), calls=%async_computation.14 | async-start | bytes 23674880 | tf_op jit(solution)/shard_map/reduce_scatter | solution.py:225
  721.4 539.9 %all-reduce.13.cloned.1.call-start = ((), (), s32[]{:S(2)}) async-start(), calls=%async_computation.19 | async-start | bytes 10027008
  794.1 593.7 %reduce-scatter.23.cloned.1.call-start = ((), (), s32[]{:S(2)}) async-start(), calls=%async_computation.17 | async-start | bytes 7520256
  943.1 572.1 %reduce-scatter.25.cloned.1.call-start = ((), (), s32[]{:S(2)}) async-start(), calls=%async_computation.18 | async-start | bytes 7520256
  1085.7 452.5 %all-gather.24.cloned.1.call-start = ((), (), s32[]{:S(2)}) async-start(), calls=%async_computation.16 | async-start | bytes 2437120 | tf_op jit(solution)/shard_map/all_gather | solution.py:238
  1102.9 163.2 %copy-start.38 = (f32[1088]{0:T(1024)S(1)}, f32[1088]{0:T(1024)}, u32[]{:S(2)}) copy-start(f32[1088]{0:T(1024)} %get-tuple-element.210) | copy-start | bytes 13060
  1106.3 188.0 %slice-start.2 = ((s8[4456448]{0:T(1024)(128)(4,1)}), s8[262144]{0:T(1024)(128)(4,1)S(1)}, s32[]{:S(2)}) async-start(s8[4456448]{0:T(1024)(128)(4,1)} %bitcast.214), calls=%async_computation.22 | async-start | bytes 524288
  1266.0 300.9 %all-gather.20.cloned.1.call-start = ((), (), s32[]{:S(2)}) async-start(), calls=%async_computation.13 | async-start | bytes 3481600 | tf_op jit(solution)/shard_map/all_gather | solution.py:240
  1266.1 28.2 %slice-start.3 = ((s8[4456448]{0:T(1024)(128)(4,1)}), s8[4194304]{0:T(1024)(128)(4,1)S(1)}, s32[]{:S(2)}) async-start(s8[4456448]{0:T(1024)(128)(4,1)} %bitcast.214), calls=%async_computation.23 | async-start | bytes 8388608
  1390.1 205.4 %all-gather.22.cloned.1.call-start = ((), (), s32[]{:S(2)}) async-start(), calls=%async_computation.15 | async-start | bytes 3481600 | tf_op jit(solution)/shard_map/all_gather | solution.py:241
  1399.1 64.3 %copy-start.35 = (f32[544]{0:T(1024)S(1)}, f32[544]{0:T(1024)}, u32[]{:S(2)}) copy-start(f32[544]{0:T(1024)} %param.43) | copy-start | bytes 6532
  1399.1 64.3 %copy-start.44 = (f32[544]{0:T(1024)S(1)}, f32[544]{0:T(1024)}, u32[]{:S(2)}) copy-start(f32[544]{0:T(1024)} %param.44) | copy-start | bytes 6532
  1399.1 64.3 %copy-start.45 = (f32[544]{0:T(1024)S(1)}, f32[544]{0:T(1024)}, u32[]{:S(2)}) copy-start(f32[544]{0:T(1024)} %param.45) | copy-start | bytes 6532
  1399.1 64.9 %copy-start.21 = (f32[8,136]{1,0:T(8,128)S(1)}, f32[8,136]{1,0:T(8,128)}, u32[]{:S(2)}) copy-start(f32[8,136]{1,0:T(8,128)} %param.40) | copy-start | bytes 13060
  1399.2 64.9 %copy-start.36 = (f32[8,136]{1,0:T(8,128)S(1)}, f32[8,136]{1,0:T(8,128)}, u32[]{:S(2)}) copy-start(f32[8,136]{1,0:T(8,128)} %param.41) | copy-start | bytes 13060
  1399.2 64.9 %copy-start.37 = (f32[8,136]{1,0:T(8,128)S(1)}, f32[8,136]{1,0:T(8,128)}, u32[]{:S(2)}) copy-start(f32[8,136]{1,0:T(8,128)} %param.42) | copy-start | bytes 13060
  (39 other events, 197.2 us)
Sparse Core Ops, SparseCore 0:
  10.8 114.9 all-gather.11
  128.5 51.7 all-gather.13
  183.1 143.7 all-gather.15
  329.6 143.4 all-gather.17
  547.4 48.0 reduce-scatter.16
  679.7 114.2 reduce-scatter.14
  796.8 139.8 reduce-scatter.18
  939.3 139.8 reduce-scatter.20
  1083.4 177.8 all-reduce.12
  1265.2 122.5 reduce-scatter.22
  1391.9 123.2 reduce-scatter.24
  1517.3 20.8 all-gather.23
  1540.4 26.4 all-gather.19
  1569.0 26.4 all-gather.21
where the time goes:
time: 1620 us
  waiting for transfers between devices  884 us (55%)
  matrix products  308 us (19%)
  local copies, waits for them, and re-layouts  156 us (10%)
  blocking collectives  142 us (9%)
  other arithmetic  108 us (7%)
  between operations  18.1 us (1%)
    unnamed x17, waiting for transfers between devices  279 us
    reduce_scatter x1, waiting for transfers between devices, per_device(): lax.psum_scatter(up_grad, 'dp', scatter_dimension=0, tiled=True)  143 us
    reduce_scatter x1, waiting for transfers between devices, per_device(): lax.psum_scatter(down_grad, 'dp', scatter_dimension=1, tiled=True)  136 us
    all_gather x1, waiting for transfers between devices, collect(): lax.all_gather(low_shards[3], 'fsdp', axis=0, tiled=True)  125 us
    unnamed x3, blocking collectives  88.7 us
    all_gather x1, waiting for transfers between devices, collect(): lax.all_gather(low_shards[2], 'fsdp', axis=1, tiled=True)  86.2 us
    unnamed x136, local copies, waits for them, and re-layouts  85.6 us
    reduce_scatter x1, waiting for transfers between devices, per_device(): lax.psum_scatter(qkv_grad, 'dp', scatter_dimension=1, tiled=True)  72.6 us
  transfers between devices with their start and end apart: 14, of which 12 were waited for; matrix products, arithmetic and copies ran while one was open for 29% of the time, Pallas kernels for 0%

commit v1 on v0

v1 whole, which is shorter than its diff:
```python
import functools
import math

import jax
import jax.numpy as jnp
from jax import lax
from jax.experimental import pallas as pl
from jax.experimental.pallas import tpu as pltpu
from jax.sharding import PartitionSpec as P

D = 1088
HEADS = 17
HDIM = 64
BLOCK = 512
STEP = 10
EXTRA = 8

norm_eps = 1e-05
beta_first = 0.9
beta_second = 0.999
adam_floor = 1e-08
step_rates = (0.05, 0.2, 0.05, 0.03, 0.5, 0.3)
decay_rates = (0.1, 0.1, 0.1, 0.1, 0.0, 0.0)

AXES = ("fsdp", "dp")
f32 = jnp.float32
bf16 = jnp.bfloat16


class Grid:
    def __init__(self):
        self.shards = lax.axis_size("fsdp")
        self.replicas = lax.axis_size("dp")
        self.zs = self.shards // 2
        self.ys = self.replicas // 2
        f, r = lax.axis_index("fsdp"), lax.axis_index("dp")
        self.z, self.x = f // 2, f % 2
        self.y, self.c = r // 2, r % 2
        self.r = r

    def move(self, value, dz=0, dx=0, dy=0, dc=0):
        pairs = []
        for z in range(self.zs):
            for x in range(2):
                for y in range(2):
                    for c in range(2):
                        here = (2 * z + x) * 4 + 2 * y + c
                        there = (2 * ((z + dz) % self.zs) + (x ^ dx)) * 4 + 2 * (y ^ dy) + (c ^ dc)
                        pairs.append((here, there))
        return lax.ppermute(value, AXES, pairs)


def after(value, *others):
    return lax.optimization_barrier((value,) + others)[0]


def take(value, at, axis=0):
    return lax.dynamic_index_in_dim(value, at, axis, keepdims=False)


def assemble_kernel(zs, *refs):
    pieces, out, sem = refs[:-2], refs[-2], refs[-1]
    f, r = lax.axis_index("fsdp"), lax.axis_index("dp")
    z, x, y, c = f // 2, f % 2, r // 2, r % 2
    copies = []
    number = 0
    for dc in range(2):
        for dy in range(2):
            for dx in range(2):
                for half in range(2):
                    piece = pieces[number]
                    number += 1
                    for k in range(zs // 2):
                        at_z = lax.rem(z - (half * (zs // 2) + k) + zs, zs)
                        owner = 2 * (y ^ dy) + (c ^ dc)
                        copies.append(
                            pltpu.make_async_copy(
                                piece.at[k],
                                out.at[owner, 2 * at_z + (x ^ dx)],
                                sem,
                            )
                        )
    for copy in copies:
        copy.start()
    for copy in copies:
        copy.wait()


def assemble(grid, pieces, rows):
    return pl.pallas_call(
        functools.partial(assemble_kernel, grid.zs),
        out_shape=jax.ShapeDtypeStruct((4, grid.shards, rows, D), bf16),
        in_specs=[pl.BlockSpec(memory_space=pl.ANY)] * len(pieces),
        out_specs=pl.BlockSpec(memory_space=pl.ANY),
        scratch_shapes=[pltpu.SemaphoreType.DMA(())],
        name="assemble",
    )(*pieces)


def gather_z(grid, unit):
    got = [unit] + [grid.move(unit, dz=k) for k in range(1, grid.zs)]
    half = grid.zs // 2
    return [jnp.stack(got[:half]), jnp.stack(got[half:])]


def gather_xy(grid, halves):
    over_x = [grid.move(h, dx=1) for h in halves]
    over_y = [grid.move(h, dy=1) for h in halves]
    diagonal = [grid.move(over_y[0], dx=1), grid.move(over_x[1], dy=1)]
    return halves + over_x + over_y + diagonal


def gather_core(grid, pieces):
    return pieces + [grid.move(p, dc=1) for p in pieces]


def reduce_group(grid, grads):
    n = grads.shape[2]
    zs, half = grid.zs, grid.zs // 2
    view = grads.reshape(2, 2, zs, 2, n, D)
    z, x, y, c = grid.z, grid.x, grid.y, grid.c
    theirs = take(view, 1 - c, 1)
    mine = take(view, c, 1)
    slabs = []
    for part in range(2):
        low, high = part * half, (part + 1) * half
        got = grid.move(theirs[:, low:high], dc=1)
        total = (mine[:, low:high].astype(f32) + got.astype(f32)).astype(bf16)
        far = take(total, 1 - y, 0)
        near = take(total, y, 0)
        diagonal = take(far, 1 - x, 1)
        to_y = take(far, x, 1)
        to_x = take(near, 1 - x, 1)
        own = take(near, x, 1)
        if part == 0:
            passed = grid.move(diagonal, dx=1)
            to_y = (to_y.astype(f32) + passed.astype(f32)).astype(bf16)
        else:
            passed = grid.move(diagonal, dy=1)
            to_x = (to_x.astype(f32) + passed.astype(f32)).astype(bf16)
        got_x = grid.move(to_x, dx=1)
        got_y = grid.move(to_y, dy=1)
        slabs.append((own.astype(f32) + got_x.astype(f32) + got_y.astype(f32)).astype(bf16))
    slab = jnp.concatenate(slabs)
    total = take(slab, z).astype(f32)
    for k in range(1, zs):
        total = total + grid.move(take(slab, (z + k) % zs), dz=k).astype(f32)
    return total.astype(bf16)


def share_unit(grid, unit):
    over_c = grid.move(unit, dc=1)
    over_y = grid.move(unit, dy=1)
    over_yc = grid.move(over_y, dc=1)
    both = jnp.stack([unit, over_c, over_y, over_yc])
    return [take(both, jnp.bitwise_xor(grid.r, r)) for r in range(4)]


def reduce_small(grid, value):
    value = value + grid.move(value, dc=1)
    value = value + grid.move(value, dy=1)
    value = value + grid.move(value, dx=1)
    parts = [value] + [grid.move(value, dz=k) for k in range(1, grid.zs)]
    return sum(parts[1:], parts[0])


def norm_forward(values, scales, offset):
    center = values - jnp.mean(values, axis=-1, keepdims=True)
    inverse = lax.rsqrt(jnp.mean(center * center, axis=-1, keepdims=True) + norm_eps)
    norm_hat = center * inverse
    return (norm_hat * scales + offset, norm_hat, inverse)


def norm_backward(gradient, norm_hat, inverse, scales):
    hat_grad = gradient * scales
    value_grad = inverse * (
        hat_grad
        - jnp.mean(hat_grad, axis=-1, keepdims=True)
        - norm_hat * jnp.mean(hat_grad * norm_hat, axis=-1, keepdims=True)
    )
    return (value_grad, jnp.sum(gradient * norm_hat, axis=0), jnp.sum(gradient, axis=0))


def causal_scores(queries, key_rows):
    scores = jnp.einsum("qhd,khd->hqk", queries, key_rows, preferred_element_type=f32) * (
        1.0 / math.sqrt(HDIM)
    )
    rows_at = lax.broadcasted_iota(jnp.int32, scores.shape, 1)
    cols_at = lax.broadcasted_iota(jnp.int32, scores.shape, 2)
    return jnp.where(rows_at >= cols_at, scores, -1e30)


def attend_forward(triple):
    queries, key_rows, values_in = triple
    scores = causal_scores(queries, key_rows)
    row_top = jnp.max(scores, axis=-1, keepdims=True)
    powers = jnp.exp(scores - row_top)
    row_total = jnp.sum(powers, axis=-1, keepdims=True)
    attn_probs = (powers / row_total).astype(bf16)
    context = jnp.einsum("hqk,khd->qhd", attn_probs, values_in, preferred_element_type=f32)
    return (context.astype(bf16), (row_top + jnp.log(row_total))[..., 0])


def attend_backward(pieces):
    queries, key_rows, values_in, logsum, context_grad = pieces
    scores = causal_scores(queries, key_rows)
    attn_probs = jnp.exp(scores - logsum[..., None])
    prob_grad = jnp.einsum("qhd,khd->hqk", context_grad, values_in, preferred_element_type=f32)
    values_grad = jnp.einsum(
        "hqk,qhd->khd", attn_probs.astype(bf16), context_grad, preferred_element_type=f32
    )
    inner_sum = jnp.sum(attn_probs * prob_grad, axis=-1, keepdims=True)
    score_grad = (attn_probs * (prob_grad - inner_sum)).astype(bf16)
    scale_factor = 1.0 / math.sqrt(HDIM)
    query_grad = jnp.einsum("hqk,khd->qhd", score_grad, key_rows, preferred_element_type=f32)
    keys_grad = jnp.einsum("hqk,qhd->khd", score_grad, queries, preferred_element_type=f32)
    return (
        (query_grad * scale_factor).astype(bf16),
        (keys_grad * scale_factor).astype(bf16),
        values_grad.astype(bf16),
    )


def adam_update(weight, mean_old, square_old, gradient, step_rate, decay_rate):
    mean_new = beta_first * mean_old + (1.0 - beta_first) * gradient
    square_new = beta_second * square_old + (1.0 - beta_second) * gradient * gradient
    mean_hat = mean_new / (1.0 - beta_first**STEP)
    square_hat = square_new / (1.0 - beta_second**STEP)
    weight_new = weight - step_rate * (
        mean_hat / (jnp.sqrt(square_hat) + adam_floor) + decay_rate * weight
    )
    return (weight_new, mean_new, square_new)


def per_device(
    hidden_in,
    cotangent,
    lengths,
    qkv_weight,
    qkv_mean,
    qkv_square,
    out_weight,
    out_mean,
    out_square,
    up_weight,
    up_mean,
    up_square,
    down_weight,
    down_mean,
    down_square,
    vectors,
    vectors_mean,
    vectors_square,
    upbias,
    upbias_mean,
    upbias_square,
):
    shards = (qkv_weight, out_weight, up_weight, down_weight, vectors, upbias)
    first_moments = (qkv_mean, out_mean, up_mean, down_mean, vectors_mean, upbias_mean)
    squares = (qkv_square, out_square, up_square, down_square, vectors_square, upbias_square)
    grid = Grid()
    n = D // grid.shards
    slots = hidden_in.shape[0]
    row_count = slots * BLOCK
    ff = 4 * D

    attn_units = jnp.stack(
        [qkv_weight[:, :D], qkv_weight[:, D : 2 * D], qkv_weight[:, 2 * D :], out_weight]
    )
    attn_unit = take(attn_units, grid.r).astype(bf16)
    small = jnp.concatenate([vectors.reshape(-1), upbias]).astype(bf16)
    small = jnp.pad(small, (0, EXTRA * D - small.shape[0])).reshape(EXTRA, D)
    up_unit = lax.dynamic_slice_in_dim(up_weight, grid.r * n, n, 1).astype(bf16).T
    down_unit = lax.dynamic_slice_in_dim(down_weight, grid.r * n, n, 0).astype(bf16)

    small_half = gather_z(grid, small)
    attn_half = gather_z(grid, after(attn_unit, *small_half))
    up_half = gather_z(grid, after(up_unit, *attn_half))
    down_half = gather_z(grid, after(down_unit, *up_half))
    attn_xy = gather_xy(grid, attn_half)
    attn_pieces = gather_core(grid, attn_xy)
    tied = lax.optimization_barrier(tuple(up_half) + tuple(attn_xy))
    up_xy = gather_xy(grid, list(tied[:2]))
    up_pieces = gather_core(grid, up_xy)
    tied = lax.optimization_barrier(tuple(down_half) + tuple(up_xy))
    down_xy = gather_xy(grid, list(tied[:2]))
    down_pieces = gather_core(grid, down_xy)
    attn_full = assemble(grid, attn_pieces, n)
    up_full = assemble(grid, up_pieces, n).reshape(ff, D)
    down_full = assemble(grid, down_pieces, n).reshape(ff, D)

    own = jnp.concatenate(small_half).reshape(grid.zs, EXTRA * D)[:, : 12 * n]
    other = grid.move(own, dx=1)
    pair = jnp.stack([own, other])
    pair = jnp.stack([take(pair, grid.x), take(pair, 1 - grid.x)])
    order = lax.rem(grid.z - jnp.arange(grid.zs) + grid.zs, grid.zs)
    pair = pair[:, order]
    smalls = pair.transpose(1, 0, 2).reshape(grid.shards, 12 * n)
    vec_values = (
        smalls[:, : 8 * n].reshape(grid.shards, 8, n).transpose(1, 0, 2).reshape(8, D).astype(f32)
    )
    bias_full = (
        smalls[:, 8 * n :].reshape(grid.shards, 4, n).transpose(1, 0, 2).reshape(ff).astype(f32)
    )

    attn_full = attn_full.reshape(4, D, D)
    qkv_full, out_full = attn_full[:3], attn_full[3]

    flat_in = hidden_in.reshape(row_count, D).astype(f32)
    positions = jnp.arange(BLOCK, dtype=jnp.int32)
    row_valid = (positions[None, :] < lengths[:, None]).astype(f32).reshape(row_count, 1)
    normed_one, hat_one, inv_one = norm_forward(flat_in, vec_values[0], vec_values[1])
    normed_low = normed_one.astype(bf16)
    bias_rows = jnp.stack([vec_values[2], jnp.zeros((D,), f32), vec_values[3]])
    qkv_rows = [
        (
            jnp.dot(normed_low, qkv_full[i], preferred_element_type=f32) + bias_rows[i]
        ).astype(bf16).reshape(slots, BLOCK, HEADS, HDIM)
        for i in range(3)
    ]
    context, logsum = lax.map(attend_forward, tuple(qkv_rows))
    context_flat = context.reshape(row_count, D)
    residual = (
        flat_in + jnp.dot(context_flat, out_full, preferred_element_type=f32) + vec_values[4]
    )
    normed_two, hat_two, inv_two = norm_forward(residual, vec_values[5], vec_values[6])
    second_low = normed_two.astype(bf16)
    up_pre = jnp.einsum("nd,fd->nf", second_low, up_full, preferred_element_type=f32) + bias_full
    active, gelu_back = jax.vjp(lambda pre_act: jax.nn.gelu(pre_act, approximate=True), up_pre)
    active_low = active.astype(bf16)
    down_out = jnp.dot(active_low, down_full, preferred_element_type=f32) + vec_values[7]
    output = ((residual + down_out) * row_valid).astype(bf16).reshape(slots, BLOCK, D)

    grad_out = cotangent.reshape(row_count, D).astype(f32) * row_valid
    grad_low = grad_out.astype(bf16)

    def weight_grad(left, right):
        return jnp.einsum("nf,nd->fd", left, right, preferred_element_type=f32).astype(bf16)

    down_grad = weight_grad(active_low, grad_low)
    down_unit_grad = reduce_group(grid, down_grad.reshape(4, grid.shards, n, D))
    down_bias_grad = jnp.sum(grad_out, axis=0)
    active_grad = jnp.einsum("nd,fd->nf", grad_low, down_full, preferred_element_type=f32)
    up_low = gelu_back(active_grad)[0].astype(bf16)
    up_grad = weight_grad(up_low, second_low)
    up_unit_grad = reduce_group(grid, up_grad.reshape(4, grid.shards, n, D))
    upbias_grad = jnp.sum(up_low.astype(f32), axis=0)
    second_grad = jnp.dot(up_low, up_full, preferred_element_type=f32)
    resid_norm_grad, scale_two_grad, offset_two_grad = norm_backward(
        second_grad, hat_two, inv_two, vec_values[5]
    )
    resid_grad = grad_out + resid_norm_grad
    branch_low = resid_grad.astype(bf16)
    out_grad = weight_grad(context_flat, branch_low)
    out_bias_grad = jnp.sum(branch_low.astype(f32), axis=0)
    context_grad = jnp.einsum("ne,de->nd", branch_low, out_full, preferred_element_type=f32)
    context_grad = context_grad.astype(bf16).reshape(slots, BLOCK, HEADS, HDIM)
    rows_grad = lax.map(attend_backward, tuple(qkv_rows) + (logsum, context_grad))
    rows_grad = [part.reshape(row_count, D) for part in rows_grad]
    attn_grad = jnp.stack([weight_grad(normed_low, part) for part in rows_grad] + [out_grad])
    attn_unit_grad = reduce_group(grid, attn_grad.reshape(4, grid.shards, n, D))
    normed_grad = sum(
        jnp.einsum("ne,de->nd", rows_grad[i], qkv_full[i], preferred_element_type=f32)
        for i in range(3)
    )
    input_norm_grad, scale_one_grad, offset_one_grad = norm_backward(
        normed_grad, hat_one, inv_one, vec_values[0]
    )
    input_grad = (resid_grad + input_norm_grad).reshape(slots, BLOCK, D)
    small_grad = jnp.concatenate(
        [
            jnp.stack(
                [
                    scale_one_grad,
                    offset_one_grad,
                    jnp.sum(rows_grad[0].astype(f32), axis=0),
                    jnp.sum(rows_grad[2].astype(f32), axis=0),
                    out_bias_grad,
                    scale_two_grad,
                    offset_two_grad,
                    down_bias_grad,
                ]
            ),
            upbias_grad.reshape(4, D),
        ]
    )
    small_grad = reduce_small(grid, small_grad)
    small_own = lax.dynamic_slice_in_dim(small_grad, (2 * grid.z + grid.x) * n, n, 1)

    down_parts = share_unit(grid, down_unit_grad)
    up_parts = share_unit(grid, up_unit_grad)
    attn_parts = share_unit(grid, attn_unit_grad)
    reduced = (
        jnp.concatenate(attn_parts[:3], axis=1).astype(f32),
        attn_parts[3].astype(f32),
        jnp.concatenate(up_parts).T.astype(f32),
        jnp.concatenate(down_parts).astype(f32),
        small_own[:8],
        small_own[8:].reshape(-1),
    )
    updates = []
    for group_index in range(6):
        updates.extend(
            adam_update(
                shards[group_index],
                first_moments[group_index],
                squares[group_index],
                reduced[group_index],
                step_rates[group_index],
                decay_rates[group_index],
            )
        )
    return (output, input_grad) + tuple(updates)


def solution(mesh):
    tokens = P(("fsdp", "dp"), None, None)
    rows, columns = P("fsdp", None), P(None, "fsdp")
    state = (rows,) * 6 + (columns,) * 3 + (rows,) * 3 + (columns,) * 3 + (P("fsdp"),) * 3
    return jax.shard_map(
        per_device,
        mesh=mesh,
        in_specs=(tokens, tokens, P(("fsdp", "dp"))) + state,
        out_specs=(tokens, tokens) + state,
        check_vma=False,
    )
```

time: 1620 us -> 1900 us (1.17)
  Pallas kernels: 0 us -> 915 us
  waiting for transfers between devices: 884 us -> 213 us
  blocking collectives: 142 us -> 0 us
  starting transfers between devices: 0.58 us -> 128 us
  local copies, waits for them, and re-layouts: 156 us -> 194 us
  other arithmetic: 108 us -> 140 us
    pallas_call x0 -> x3, Pallas kernels: none -> 915 us  [assemble(): pl.pallas_call(functools.partial(assemble_kernel, grid.zs), out_shape=jax...]
    reduce_scatter x4 -> x0, waiting for transfers between devices: 351 us -> none  [the longest x1 143 us: per_device(): lax.psum_scatter(up_grad, 'dp', scatter_dimension=0, tiled=True)]
    unnamed x17 -> x0, waiting for transfers between devices: 279 us -> none
    all_gather x7 -> x0, waiting for transfers between devices: 254 us -> none  [the longest x1 125 us: collect(): lax.all_gather(low_shards[3], 'fsdp', axis=0, tiled=True)]
    ppermute x0 -> x103, waiting for transfers between devices: none -> 213 us  [move(): return lax.ppermute(value, AXES, pairs)]
    ppermute x0 -> x103, starting transfers between devices: none -> 128 us  [move(): return lax.ppermute(value, AXES, pairs)]
    unnamed x3 -> x0, blocking collectives: 88.7 us -> none
    unnamed x136 -> x257, local copies, waits for them, and re-layouts: 85.6 us -> 22.6 us
  transfers between devices with their start and end apart: 14 -> 103, of which waited for: 12 -> 31; matrix products, arithmetic and copies ran while one was open for 29% -> 31% of each run, Pallas kernels for 0% -> 48%
where the time goes in v1:
time: 1900 us; the launch traced here: 1890 us
  Pallas kernels  915 us (48%)
  matrix products  301 us (16%)
  waiting for transfers between devices  213 us (11%)
  local copies, waits for them, and re-layouts  194 us (10%)
  other arithmetic  140 us (7%)
  starting transfers between devices  128 us (7%)
    pallas_call x3, Pallas kernels, assemble(): pl.pallas_call(functools.partial(assemble_kernel, grid.zs), out_shape=jax...  915 us
    ppermute x103, waiting for transfers between devices, move(): return lax.ppermute(value, AXES, pairs)  213 us
    ppermute x103, starting transfers between devices, move(): return lax.ppermute(value, AXES, pairs)  128 us
    dot_general x6, matrix products, weight_grad(): jnp.einsum('nf,nd->fd', left, right, preferred_element_type=f32)  54.3 us
    dot_general x4, matrix products, causal_scores(): jnp.einsum('qhd,khd->hqk', queries, key_rows, preferred_element_type=f32)  43 us
  transfers between devices with their start and end apart: 103, of which 31 were waited for; matrix products, arithmetic and copies ran while one was open for 31% of the time, Pallas kernels for 48%

profile of v1, /device:TPU:0, one launch (start us, length us, event | category | flops | bytes accessed | tf_op | source)
XLA Modules:
  0.0 1893.9 jit_solution(15012245274995062059)
XLA Ops:
  118.6 10.2 collective-permute-done.10.refs_5_
  130.4 11.5 collective-permute-done.12.refs_7_
  158.2 304.9 %assemble.3 = bf16[4,8,136,1088]{3,2,1,0:T(8,128)(2,1)} custom-call(bf16[2,136,1088]{2,1,0:T(8,128)(2,1)} %copy-done.24, bf16[2,136,1088]{2,1,0:T(8,128)(2,1)} %copy-done.23, bf16[2,136,1088]{2,1,0:T(8,128)(2,1)} %collective-permute-done.7.refs_2_, bf16[2,136,1088]{2,1,0:T(8,128)(2,1)} %collective-permute-done.8.refs_3_, ...), custom_call_target="tpu_custom_call" | custom-call | tf_op jit(solution)/shard_map/assemble/pallas_call | solution.py:90
  518.0 55.6 %while.26 = (s32[]{:T(128)}, bf16[2,512,17,64]{1,3,2,0:T(8,128)(2,1)}, f32[2,17,512]{2,1,0:T(8,128)}, bf16[2,512,17,64]{1,3,2,0:T(8,128)(2,1)}, bf16[2,512,17,64...) while((s32[]{:T(128)}, bf16[2,512,17,64]{1,3,2,0:T(8,128)(2,1)}, ...), condition=%wide.region_5.6_spmd, body=%wide.region_2.5_spmd.sunk | while | flops 1208245760 | bytes 58228824 | solution.py:321
  596.9 12.1 collective-permute-done.29.refs_7_
  614.2 304.9 %assemble.4 = bf16[4,8,136,1088]{3,2,1,0:T(8,128)(2,1)} custom-call(bf16[2,136,1088]{2,1,0:T(8,128)(2,1)} %pad_maximum_fusion.8.refs_0_, bf16[2,136,1088]{2,1,0:T(8,128)(2,1)} %pad_maximum_fusion.9.refs_1_, bf16[2,136,1088]{2,1,0:T(8,128)(2,1)} %collective-permute-done.24.refs_2_, bf16[2,136,1088]{2,1,0:T(8,128)(2,1)} %collective-permute-done.25.refs_3_, ...), custom_call_target="tpu_custom_call" | custom-call | tf_op jit(solution)/shard_map/assemble/pallas_call | solution.py:90
  919.1 21.4 %fusion.159 = f32[1024,4352]{1,0:T(8,128)} fusion(bf16[4352,1088]{1,0:T(8,128)(2,1)} %bitcast.419, f32[1024,1088]{0,1:T(8,128)} %copy-done.10, f32[1088]{0:T(1024)S(1)} %copy-done.105, f32[1088]{0:T(1024)S(1)} %copy-done.85, f32[1024]{0:T(1024)S(1)} %add_rsqrt_fusion, f32[1024]{0:T(1024)S(1)} %broadcast_multiply_fusion.4), kind=kOutput, calls=%fused_computation.357 | convolution fusion | flops 9702801408 | bytes 31769088 | tf_op jit(solution)/shard_map/nd,fd->nf/dot_general | solution.py:328
  940.5 17.1 convolution_convert_fusion
  957.7 13.9 copy.152
  990.2 10.4 collective-permute-done.46.refs_7_
  1006.3 304.9 %assemble.5 = bf16[4,8,136,1088]{3,2,1,0:T(8,128)(2,1)} custom-call(bf16[2,136,1088]{2,1,0:T(8,128)(2,1)} %pad_maximum_fusion.10.refs_0_, bf16[2,136,1088]{2,1,0:T(8,128)(2,1)} %pad_maximum_fusion.11.refs_1_, bf16[2,136,1088]{2,1,0:T(8,128)(2,1)} %copy-done.61, bf16[2,136,1088]{2,1,0:T(8,128)(2,1)} %collective-permute-done.42.refs_3_, ...), custom_call_target="tpu_custom_call" | custom-call | tf_op jit(solution)/shard_map/assemble/pallas_call | solution.py:90
  1311.2 25.1 %convert_reduce_fusion = (f32[4352]{0:T(1024)}, bf16[1024,4352]{1,0:T(8,128)(2,1)}) fusion(f32[1024,4352]{1,0:T(8,128)} %fusion.159, f32[4352]{0:T(1024)S(1)} %copy-done.93, bf16[1024,1088]{1,0:T(8,128)(2,1)S(1)} %bitcast.435, bf16[4352,1088]{1,0:T(8,128)(2,1)} %bitcast.417), kind=kOutput, calls=%fused_computation.70 | convolution fusion | flops 9799725056 | bytes 38471680 | tf_op jit(solution)/shard_map/nd,fd->nf/dot_general | solution.py:343
  1336.3 19.5 %multiply_reduce_fusion.1 = (f32[1088]{0:T(1024)}, f32[1024]{0:T(1024)S(1)}, f32[1024]{0:T(1024)S(1)}, f32[1088]{0:T(1024)}, f32[1024,1088]{0,1:T(8,128)}) fusion(f32[1024,1088]{0,1:T(8,128)} %copy-done.10, f32[1024]{0:T(1024)S(1)} %add_rsqrt_fusion, f32[1024]{0:T(1024)S(1)} %broadcast_multiply_fusion.4, f32[1088]{0:T(1024)S(1)} %copy-done.85, ...), kind=kOutput, calls=%fused_computation.116 | convolution fusion | flops 9707253760 | bytes 27325184 | tf_op jit(solution)/shard_map/dot_general | solution.py:348
  1355.7 17.6 convolution_convert_fusion.1
  1396.8 104.8 %while.27 = (s32[]{:T(128)}, bf16[2,512,17,64]{1,3,2,0:T(8,128)(2,1)}, bf16[2,512,17,64]{1,3,2,0:T(8,128)(2,1)}, bf16[2,512,17,64]{1,3,2,0:T(8,128)(2,1)}, bf16[...) while((s32[]{:T(128)}, ...), condition=%wide.region_12.13_spmd, body=%wide.region_10.12_spmd.sunk | while | flops 2899467776 | bytes 180679904 | solution.py:358
  1397.0 10.4 fusion.240
  1407.4 12.5 multiply_reduce_fusion.9
  1419.9 12.3 multiply_convert_fusion.9
  1432.2 10.2 fusion.243
  1449.2 10.4 fusion.240
  1459.6 12.5 multiply_reduce_fusion.9
  1472.1 12.3 multiply_convert_fusion.9
  1484.4 10.2 fusion.243
  1538.8 23.7 %fusion.77 = bf16[1024,1088]{0,1:T(8,128)(2,1)} fusion(f32[1024,1088]{0,1:T(8,128)S(1)} %bitcast.413, bf16[4352,1088]{1,0:T(8,128)(2,1)} %bitcast.418, f32[1024]{0:T(1024)S(1)} %bitcast.477, f32[1088]{0:T(1024)S(1)} %copy-done.104, f32[1024,4352]{1,0:T(8,128)} %fusion.159, f32[4352]{0:T(1024)S(1)} %copy-done.94), kind=kOutput, calls=%fused_computation.134 | convolution fusion | flops 9746251776 | bytes 34006272 | tf_op jit(solution)/shard_map/dot_general | solution.py:331
  1564.7 13.9 copy.148
  1679.9 16.6 collective-permute-done.86
  1716.2 10.6 collective-permute-done.92
  1732.9 10.9 collective-permute-done.60
  1758.9 13.5 collective-permute-done.61
  1777.0 13.8 collective-permute-done.95
  1790.8 12.6 collective-permute-done.72
  1832.5 16.0 collective-permute-start.79
  (655 shorter events, 594.6 us)
Async XLA Ops:
  3.1 58.7 %collective-permute-start.2 = (bf16[8,1088]{1,0:T(8,128)(2,1)}, bf16[8,1088]{1,0:T(8,128)(2,1)}, u32[]{:S(2)}, u32[]{:S(2)}) collective-permute-start(bf16[8,1088]{1,0:T(8,128)(2,1)} %reshape.514), channel_id=1, source_target_pairs={{0,24},{1,25},{2,26},{3,27},{4,28},{5,29},{6,30},{7,31},{8,0},{9,1... | collective-permute-start | bytes 52232 | tf_op jit(solution)/shard_map/ppermute | solution.py:50
  8.1 54.5 %collective-permute-start.1 = (bf16[8,1088]{1,0:T(8,128)(2,1)}, bf16[8,1088]{1,0:T(8,128)(2,1)}, u32[]{:S(2)}, u32[]{:S(2)}) collective-permute-start(bf16[8,1088]{1,0:T(8,128)(2,1)} %reshape.514), channel_id=1, source_target_pairs={{0,16},{1,17},{2,18},{3,19},{4,20},{5,21},{6,22},{7,23},{8,24},{9,... | collective-permute-start | bytes 52232 | tf_op jit(solution)/shard_map/ppermute | solution.py:50
  10.6 29.9 %collective-permute-start.5 = (bf16[136,1088]{1,0:T(8,128)(2,1)S(1)}, bf16[136,1088]{1,0:T(8,128)(2,1)S(1)}, u32[]{:S(2)}, u32[]{:S(2)}) collective-permute-start(bf16[136,1088]{1,0:T(8,128)(2,1)S(1)} %fusion.143), channel_id=1, source_target_pairs={{0,16},{1,17},{2,18},{3,19},{4,20},{5,21},{6,22},{7,23},{8,24},{9,... | collective-permute-start | bytes 887816 | tf_op jit(solution)/shard_map/ppermute | solution.py:50
  13.1 29.1 %collective-permute-start.4 = (bf16[136,1088]{1,0:T(8,128)(2,1)S(1)}, bf16[136,1088]{1,0:T(8,128)(2,1)}, u32[]{:S(2)}, u32[]{:S(2)}) collective-permute-start(bf16[136,1088]{1,0:T(8,128)(2,1)S(1)} %fusion.143), channel_id=1, source_target_pairs={{0,8},{1,9},{2,10},{3,11},{4,12},{5,13},{6,14},{7,15},{8,16},{9,17... | collective-permute-start | bytes 887816 | tf_op jit(solution)/shard_map/ppermute | solution.py:50
  30.1 34.0 %collective-permute-start = (bf16[8,1088]{1,0:T(8,128)(2,1)}, bf16[8,1088]{1,0:T(8,128)(2,1)}, u32[]{:S(2)}, u32[]{:S(2)}) collective-permute-start(bf16[8,1088]{1,0:T(8,128)(2,1)} %reshape.514), channel_id=1, source_target_pairs={{0,8},{1,9},{2,10},{3,11},{4,12},{5,13},{6,14},{7,15},{8,16},{9,17... | collective-permute-start | bytes 52232 | tf_op jit(solution)/shard_map/ppermute | solution.py:50
  79.7 33.9 %collective-permute-start.9 = (bf16[2,136,1088]{2,1,0:T(8,128)(2,1)S(1)}, bf16[2,136,1088]{2,1,0:T(8,128)(2,1)}, u32[]{:S(2)}, u32[]{:S(2)}) collective-permute-start(bf16[2,136,1088]{2,1,0:T(8,128)(2,1)S(1)} %pad_maximum_fusion.6.refs_0_), channel_id=1, source_target_pairs={{0,2},{1,3},{2,0},{3,1},{4,6},{5,7},{6,4},{7,5},{8,10},{9,11},{10,... | collective-permute-start | bytes 1775624 | tf_op jit(solution)/shard_map/ppermute | solution.py:50
  83.6 30.2 %collective-permute-start.7 = (bf16[2,136,1088]{2,1,0:T(8,128)(2,1)S(1)}, bf16[2,136,1088]{2,1,0:T(8,128)(2,1)}, u32[]{:S(2)}, u32[]{:S(2)}) collective-permute-start(bf16[2,136,1088]{2,1,0:T(8,128)(2,1)S(1)} %pad_maximum_fusion.6.refs_0_), channel_id=1, source_target_pairs={{0,4},{1,5},{2,6},{3,7},{4,0},{5,1},{6,2},{7,3},{8,12},{9,13},{10,... | collective-permute-start | bytes 1775624 | tf_op jit(solution)/shard_map/ppermute | solution.py:50
  118.6 37.5 %collective-permute-start.16 = (bf16[2,136,1088]{2,1,0:T(8,128)(2,1)}, bf16[2,136,1088]{2,1,0:T(8,128)(2,1)}, u32[]{:S(2)}, u32[]{:S(2)}) collective-permute-start(bf16[2,136,1088]{2,1,0:T(8,128)(2,1)} %collective-permute-done.8.refs_3_), channel_id=1, source_target_pairs={{0,1},{1,0},{2,3},{3,2},{4,5},{5,4},{6,7},{7,6},{8,9},{9,8},{10,11... | collective-permute-start | bytes 1775624 | tf_op jit(solution)/shard_map/ppermute | solution.py:50
  153.8 425.3 %collective-permute-start.30 = (bf16[2,136,1088]{2,1,0:T(8,128)(2,1)}, bf16[2,136,1088]{2,1,0:T(8,128)(2,1)}, u32[]{:S(2)}, u32[]{:S(2)}) collective-permute-start(bf16[2,136,1088]{2,1,0:T(8,128)(2,1)} %pad_maximum_fusion.8.refs_0_), channel_id=1, source_target_pairs={{0,1},{1,0},{2,3},{3,2},{4,5},{5,4},{6,7},{7,6},{8,9},{9,8},{10,11... | collective-permute-start | bytes 1775624 | tf_op jit(solution)/shard_map/ppermute | solution.py:50
  154.3 425.1 %collective-permute-start.26 = (bf16[2,136,1088]{2,1,0:T(8,128)(2,1)}, bf16[2,136,1088]{2,1,0:T(8,128)(2,1)}, u32[]{:S(2)}, u32[]{:S(2)}) collective-permute-start(bf16[2,136,1088]{2,1,0:T(8,128)(2,1)} %pad_maximum_fusion.8.refs_0_), channel_id=1, source_target_pairs={{0,2},{1,3},{2,0},{3,1},{4,6},{5,7},{6,4},{7,5},{8,10},{9,11},{10,... | collective-permute-start | bytes 1775624 | tf_op jit(solution)/shard_map/ppermute | solution.py:50
  156.1 423.4 %collective-permute-start.24 = (bf16[2,136,1088]{2,1,0:T(8,128)(2,1)}, bf16[2,136,1088]{2,1,0:T(8,128)(2,1)}, u32[]{:S(2)}, u32[]{:S(2)}) collective-permute-start(bf16[2,136,1088]{2,1,0:T(8,128)(2,1)} %pad_maximum_fusion.8.refs_0_), channel_id=1, source_target_pairs={{0,4},{1,5},{2,6},{3,7},{4,0},{5,1},{6,2},{7,3},{8,12},{9,13},{10,... | collective-permute-start | bytes 1775624 | tf_op jit(solution)/shard_map/ppermute | solution.py:50
  157.6 428.6 %collective-permute-start.31 = (bf16[2,136,1088]{2,1,0:T(8,128)(2,1)}, bf16[2,136,1088]{2,1,0:T(8,128)(2,1)}, u32[]{:S(2)}, u32[]{:S(2)}) collective-permute-start(bf16[2,136,1088]{2,1,0:T(8,128)(2,1)} %pad_maximum_fusion.9.refs_1_), channel_id=1, source_target_pairs={{0,1},{1,0},{2,3},{3,2},{4,5},{5,4},{6,7},{7,6},{8,9},{9,8},{10,11... | collective-permute-start | bytes 1775624 | tf_op jit(solution)/shard_map/ppermute | solution.py:50
  157.6 423.4 %collective-permute-start.25 = (bf16[2,136,1088]{2,1,0:T(8,128)(2,1)}, bf16[2,136,1088]{2,1,0:T(8,128)(2,1)}, u32[]{:S(2)}, u32[]{:S(2)}) collective-permute-start(bf16[2,136,1088]{2,1,0:T(8,128)(2,1)} %pad_maximum_fusion.9.refs_1_), channel_id=1, source_target_pairs={{0,4},{1,5},{2,6},{3,7},{4,0},{5,1},{6,2},{7,3},{8,12},{9,13},{10,... | collective-permute-start | bytes 1775624 | tf_op jit(solution)/shard_map/ppermute | solution.py:50
  609.6 362.0 %collective-permute-start.47 = (bf16[2,136,1088]{2,1,0:T(8,128)(2,1)S(1)}, bf16[2,136,1088]{2,1,0:T(8,128)(2,1)S(1)}, u32[]{:S(2)}, u32[]{:S(2)}) collective-permute-start(bf16[2,136,1088]{2,1,0:T(8,128)(2,1)S(1)} %copy-done.26), channel_id=1, source_target_pairs={{0,1},{1,0},{2,3},{3,2},{4,5},{5,4},{6,7},{7,6},{8,9},{9,8},{10,11... | collective-permute-start | bytes 1775624 | tf_op jit(solution)/shard_map/ppermute | solution.py:50
  610.1 363.2 %collective-permute-start.43 = (bf16[2,136,1088]{2,1,0:T(8,128)(2,1)S(1)}, bf16[2,136,1088]{2,1,0:T(8,128)(2,1)}, u32[]{:S(2)}, u32[]{:S(2)}) collective-permute-start(bf16[2,136,1088]{2,1,0:T(8,128)(2,1)S(1)} %copy-done.26), channel_id=1, source_target_pairs={{0,2},{1,3},{2,0},{3,1},{4,6},{5,7},{6,4},{7,5},{8,10},{9,11},{10,... | collective-permute-start | bytes 1775624 | tf_op jit(solution)/shard_map/ppermute | solution.py:50
  610.4 362.9 %collective-permute-start.41 = (bf16[2,136,1088]{2,1,0:T(8,128)(2,1)S(1)}, bf16[2,136,1088]{2,1,0:T(8,128)(2,1)S(1)}, u32[]{:S(2)}, u32[]{:S(2)}) collective-permute-start(bf16[2,136,1088]{2,1,0:T(8,128)(2,1)S(1)} %copy-done.26), channel_id=1, source_target_pairs={{0,4},{1,5},{2,6},{3,7},{4,0},{5,1},{6,2},{7,3},{8,12},{9,13},{10,... | collective-permute-start | bytes 1775624 | tf_op jit(solution)/shard_map/ppermute | solution.py:50
  612.0 370.3 %collective-permute-start.48 = (bf16[2,136,1088]{2,1,0:T(8,128)(2,1)S(1)}, bf16[2,136,1088]{2,1,0:T(8,128)(2,1)}, u32[]{:S(2)}, u32[]{:S(2)}) collective-permute-start(bf16[2,136,1088]{2,1,0:T(8,128)(2,1)S(1)} %copy-done.25), channel_id=1, source_target_pairs={{0,1},{1,0},{2,3},{3,2},{4,5},{5,4},{6,7},{7,6},{8,9},{9,8},{10,11... | collective-permute-start | bytes 1775624 | tf_op jit(solution)/shard_map/ppermute | solution.py:50
  613.7 361.2 %collective-permute-start.42 = (bf16[2,136,1088]{2,1,0:T(8,128)(2,1)S(1)}, bf16[2,136,1088]{2,1,0:T(8,128)(2,1)}, u32[]{:S(2)}, u32[]{:S(2)}) collective-permute-start(bf16[2,136,1088]{2,1,0:T(8,128)(2,1)S(1)} %copy-done.25), channel_id=1, source_target_pairs={{0,4},{1,5},{2,6},{3,7},{4,0},{5,1},{6,2},{7,3},{8,12},{9,13},{10,... | collective-permute-start | bytes 1775624 | tf_op jit(solution)/shard_map/ppermute | solution.py:50
  1004.1 642.0 %collective-permute-start.83 = (bf16[2,2,2,136,1088]{4,3,1,2,0:T(8,128)(2,1)}, bf16[2,2,2,136,1088]{4,3,1,2,0:T(8,128)(2,1)}, u32[]{:S(2)}, u32[]{:S(2)}) collective-permute-start(bf16[2,2,2,136,1088]{4,3,1,2,0:T(8,128)(2,1)} %copy.166), channel_id=1, source_target_pairs={{0,1},{1,0},{2,3},{3,2},{4,5},{5,4},{6,7},{7,6},{8,9},{9,8},{10,11... | collective-permute-start | bytes 7102472 | tf_op jit(solution)/shard_map/ppermute | solution.py:50
  1005.7 644.3 %collective-permute-start.87 = (bf16[2,2,2,136,1088]{4,3,2,1,0:T(8,128)(2,1)}, bf16[2,2,2,136,1088]{4,3,2,1,0:T(8,128)(2,1)}, u32[]{:S(2)}, u32[]{:S(2)}) collective-permute-start(bf16[2,2,2,136,1088]{4,3,2,1,0:T(8,128)(2,1)} %get-tuple-element.341), channel_id=1, source_target_pairs={{0,1},{1,0},{2,3},{3,2},{4,5},{5,4},{6,7},{7,6},{8,9},{9,8},{10,11... | collective-permute-start | bytes 7102472 | tf_op jit(solution)/shard_map/ppermute | solution.py:50
  1645.5 55.9 %collective-permute-start.73 = (bf16[2,2,2,136,1088]{4,3,2,1,0:T(8,128)(2,1)}, bf16[2,2,2,136,1088]{4,3,2,1,0:T(8,128)(2,1)}, u32[]{:S(2)}, u32[]{:S(2)}) collective-permute-start(bf16[2,2,2,136,1088]{4,3,2,1,0:T(8,128)(2,1)} %get-tuple-element.343), channel_id=1, source_target_pairs={{0,1},{1,0},{2,3},{3,2},{4,5},{5,4},{6,7},{7,6},{8,9},{9,8},{10,11... | collective-permute-start | bytes 7102472 | tf_op jit(solution)/shard_map/ppermute | solution.py:50
  1666.6 31.2 %collective-permute-start.90 = (bf16[2,136,1088]{2,1,0:T(8,128)(2,1)}, bf16[2,136,1088]{2,1,0:T(8,128)(2,1)S(1)}, u32[]{:S(2)}, u32[]{:S(2)}) collective-permute-start(bf16[2,136,1088]{2,1,0:T(8,128)(2,1)} %get-tuple-element.350), channel_id=1, source_target_pairs={{0,2},{1,3},{2,0},{3,1},{4,6},{5,7},{6,4},{7,5},{8,10},{9,11},{10,... | collective-permute-start | bytes 1775624 | tf_op jit(solution)/shard_map/ppermute | solution.py:50
  1697.8 79.1 %collective-permute-start.70 = (bf16[2,136,1088]{2,1,0:T(8,128)(2,1)S(1)}, bf16[2,136,1088]{2,1,0:T(8,128)(2,1)}, u32[]{:S(2)}, u32[]{:S(2)}) collective-permute-start(bf16[2,136,1088]{2,1,0:T(8,128)(2,1)S(1)} %get-tuple-element.355), channel_id=1, source_target_pairs={{0,4},{1,5},{2,6},{3,7},{4,0},{5,1},{6,2},{7,3},{8,12},{9,13},{10,... | collective-permute-start | bytes 1775624 | tf_op jit(solution)/shard_map/ppermute | solution.py:50
  1699.4 30.8 %collective-permute-start.71 = (bf16[2,136,1088]{2,1,0:T(8,128)(2,1)S(1)}, bf16[2,136,1088]{2,1,0:T(8,128)(2,1)}, u32[]{:S(2)}, u32[]{:S(2)}) collective-permute-start(bf16[2,136,1088]{2,1,0:T(8,128)(2,1)S(1)} %get-tuple-element.356), channel_id=1, source_target_pairs={{0,4},{1,5},{2,6},{3,7},{4,0},{5,1},{6,2},{7,3},{8,12},{9,13},{10,... | collective-permute-start | bytes 1775624 | tf_op jit(solution)/shard_map/ppermute | solution.py:50
  1714.4 33.6 %collective-permute-start.74 = (bf16[2,136,1088]{2,1,0:T(8,128)(2,1)S(1)}, bf16[2,136,1088]{2,1,0:T(8,128)(2,1)S(1)}, u32[]{:S(2)}, u32[]{:S(2)}) collective-permute-start(bf16[2,136,1088]{2,1,0:T(8,128)(2,1)S(1)} %get-tuple-element.353), channel_id=1, source_target_pairs={{0,2},{1,3},{2,0},{3,1},{4,6},{5,7},{6,4},{7,5},{8,10},{9,11},{10,... | collective-permute-start | bytes 1775624 | tf_op jit(solution)/shard_map/ppermute | solution.py:50
  1743.8 30.6 %collective-permute-start.56 = (bf16[2,136,1088]{2,1,0:T(8,128)(2,1)S(1)}, bf16[2,136,1088]{2,1,0:T(8,128)(2,1)S(1)}, u32[]{:S(2)}, u32[]{:S(2)}) collective-permute-start(bf16[2,136,1088]{2,1,0:T(8,128)(2,1)S(1)} %get-tuple-element.359), channel_id=1, source_target_pairs={{0,4},{1,5},{2,6},{3,7},{4,0},{5,1},{6,2},{7,3},{8,12},{9,13},{10,... | collective-permute-start | bytes 1775624 | tf_op jit(solution)/shard_map/ppermute | solution.py:50
  1757.2 51.8 %collective-permute-start.76 = (bf16[2,136,1088]{2,1,0:T(8,128)(2,1)S(1)}, bf16[2,136,1088]{2,1,0:T(8,128)(2,1)S(1)}, u32[]{:S(2)}, u32[]{:S(2)}) collective-permute-start(bf16[2,136,1088]{2,1,0:T(8,128)(2,1)S(1)} %get-tuple-element.354), channel_id=1, source_target_pairs={{0,2},{1,3},{2,0},{3,1},{4,6},{5,7},{6,4},{7,5},{8,10},{9,11},{10,... | collective-permute-start | bytes 1775624 | tf_op jit(solution)/shard_map/ppermute | solution.py:50
  1774.4 28.9 %collective-permute-start.72 = (bf16[2,136,1088]{2,1,0:T(8,128)(2,1)S(1)}, bf16[2,136,1088]{2,1,0:T(8,128)(2,1)S(1)}, u32[]{:S(2)}, u32[]{:S(2)}) collective-permute-start(bf16[2,136,1088]{2,1,0:T(8,128)(2,1)S(1)} %fusion.94), channel_id=1, source_target_pairs={{0,2},{1,3},{2,0},{3,1},{4,6},{5,7},{6,4},{7,5},{8,10},{9,11},{10,... | collective-permute-start | bytes 1775624 | tf_op jit(solution)/shard_map/ppermute | solution.py:50
  1774.8 37.7 %collective-permute-start.75 = (bf16[2,136,1088]{2,1,0:T(8,128)(2,1)S(1)}, bf16[2,136,1088]{2,1,0:T(8,128)(2,1)S(1)}, u32[]{:S(2)}, u32[]{:S(2)}) collective-permute-start(bf16[2,136,1088]{2,1,0:T(8,128)(2,1)S(1)} %fusion.91), channel_id=1, source_target_pairs={{0,4},{1,5},{2,6},{3,7},{4,0},{5,1},{6,2},{7,3},{8,12},{9,13},{10,... | collective-permute-start | bytes 1775624 | tf_op jit(solution)/shard_map/ppermute | solution.py:50
  1776.9 85.7 %collective-permute-start.94 = (bf16[136,1088]{1,0:T(8,128)(2,1)S(1)}, bf16[136,1088]{1,0:T(8,128)(2,1)S(1)}, u32[]{:S(2)}, u32[]{:S(2)}) collective-permute-start(bf16[136,1088]{1,0:T(8,128)(2,1)S(1)} %fusion.111), channel_id=1, source_target_pairs={{0,1},{1,0},{2,3},{3,2},{4,5},{5,4},{6,7},{7,6},{8,9},{9,8},{10,11... | collective-permute-start | bytes 887816 | tf_op jit(solution)/shard_map/ppermute | solution.py:50
  1790.8 71.9 %collective-permute-start.96 = (bf16[136,1088]{1,0:T(8,128)(2,1)S(1)}, bf16[136,1088]{1,0:T(8,128)(2,1)S(1)}, u32[]{:S(2)}, u32[]{:S(2)}) collective-permute-start(bf16[136,1088]{1,0:T(8,128)(2,1)S(1)} %collective-permute-done.95), channel_id=1, source_target_pairs={{0,1},{1,0},{2,3},{3,2},{4,5},{5,4},{6,7},{7,6},{8,9},{9,8},{10,11... | collective-permute-start | bytes 887816 | tf_op jit(solution)/shard_map/ppermute | solution.py:50
  1819.0 29.8 %collective-permute-start.77 = (bf16[136,1088]{1,0:T(8,128)(2,1)S(1)}, bf16[136,1088]{1,0:T(8,128)(2,1)S(1)}, u32[]{:S(2)}, u32[]{:S(2)}) collective-permute-start(bf16[136,1088]{1,0:T(8,128)(2,1)S(1)} %get-tuple-element.377), channel_id=1, source_target_pairs={{0,8},{1,9},{2,10},{3,11},{4,12},{5,13},{6,14},{7,15},{8,16},{9,17... | collective-permute-start | bytes 887816 | tf_op jit(solution)/shard_map/ppermute | solution.py:50
  (203 other events, 4261.5 us)
